TPU v7x, 256 devices: a whole 4x4x8 slice. The times are simulated.
256 devices in a mesh: section: 4 (over y_lo, core), expert: 32 (over z, x), dp: 2 (over y_hi).
Axes of the slice: x: 4, y: 4 (y_hi: 2, y_lo: 2; y = y_hi * 2 + y_lo), z: 8, core: 2. Of those that a mesh axis runs over, the one named last changes fastest.
Arguments:
- fwd_in: bfloat16 [4, 8192, 2048], P('section', ('expert', 'dp')), may hold values from -6 to 6
- saved_in: bfloat16 [4, 8192, 2048], P('section', ('expert', 'dp')), may hold values from -6 to 6
- out_grad: bfloat16 [4, 8192, 2048], P('section', ('expert', 'dp')), may hold values from -6 to 6
- gain: bfloat16 [4, 2048], P('section'), may hold values from 0.25 to 1.75
- router: bfloat16 [4, 2048, 32], P('section'), may hold values from -0.25 to 0.25
- w_gate: bfloat16 [4, 32, 2048, 704], P('section', 'expert', None, 'dp'), may hold values from -0.125 to 0.125
- w_up: bfloat16 [4, 32, 2048, 704], P('section', 'expert', None, 'dp'), may hold values from -0.125 to 0.125
- w_down: bfloat16 [4, 32, 704, 2048], P('section', 'expert', 'dp'), may hold values from -0.21875 to 0.21875
- routes_fwd: int32 [4, 8192, 2], P('section', ('expert', 'dp')), may hold values from 0 to 31, all different within a row; in each aligned block of 128 rows (0 to 127, 128 to 255, ..., all dimensions but the last counted through in order) at most 12 rows name the same one
- routes_bwd: int32 [4, 8192, 2], P('section', ('expert', 'dp')), may hold values from 0 to 31, all different within a row; in each aligned block of 128 rows (0 to 127, 128 to 255, ..., all dimensions but the last counted through in order) at most 12 rows name the same one
Outputs:
- sent_fwd: bfloat16 [4, 8192, 2048], P('section', ('expert', 'dp'))
- sent_bwd: bfloat16 [4, 8192, 2048], P('section', ('expert', 'dp'))
- grad_gate: bfloat16 [4, 32, 2048, 704], P('section', 'expert', None, 'dp')
- grad_up: bfloat16 [4, 32, 2048, 704], P('section', 'expert', None, 'dp')
- grad_down: bfloat16 [4, 32, 704, 2048], P('section', 'expert', 'dp')
- grad_router: float32 [4, 2048, 32], P('section')
- grad_gain: float32 [4, 2048], P('section')
Inputs may be any that keep to these rules, and one draw needn't show every extreme that they name: `routes_fwd`: each token names 2 different experts. In each aligned block of 128 tokens (the tokens of one device) no expert is named by more than 12 tokens, and in every draw some block has an expert named by exactly 12. `routes_bwd`: as for routes_fwd.
All inputs are finite; a program needn't handle non-finite values.
Results may differ from a plain program's by a relative error of at most 0.019.
Values may be sent and summed in bfloat16 or wider, within the bound.
A program may use at most 128 MiB of HBM per device.

v0:
```python
import jax
import jax.numpy as jnp
from jax import lax
from jax.sharding import PartitionSpec as P

EPS = 1e-06


def shifted(value, axis, steps):
    count = lax.axis_size(axis)
    pairs = [(source, (source + steps) % count) for source in range(count)]
    return lax.ppermute(value, axis, pairs)


def norm_rows(inputs, gain_row):
    as_float = inputs.astype(jnp.float32)
    inverse = lax.rsqrt(jnp.mean(as_float * as_float, axis=-1, keepdims=True) + EPS)
    normed = (as_float * inverse * gain_row.astype(jnp.float32)).astype(jnp.bfloat16)
    return (as_float, inverse, normed)


def router_gates(normed, router_mat, routes):
    logits = jnp.dot(normed, router_mat, preferred_element_type=jnp.float32)
    experts = router_mat.shape[1]
    selector = (routes[:, :, None] == jnp.arange(experts, dtype=jnp.int32)[None, None, :]).astype(
        jnp.float32
    )
    chosen = jnp.sum(selector * logits[:, None, :], axis=-1)
    return (jax.nn.sigmoid(chosen), selector)


def route_slots(routes, experts, capacity):
    count = routes.shape[0] * routes.shape[1]
    flat = routes.reshape(count)
    onehot = (flat[:, None] == jnp.arange(experts, dtype=jnp.int32)[None, :]).astype(jnp.int32)
    before = jnp.cumsum(onehot, axis=0) - onehot
    slots = jnp.sum(before * onehot, axis=1)
    return flat * capacity + slots


def expert_result(rows_in, gate_weight, up_weight, down_weight):
    pre_gate = jnp.dot(rows_in, gate_weight, preferred_element_type=jnp.float32)
    pre_up = jnp.dot(rows_in, up_weight, preferred_element_type=jnp.float32)
    hidden = (pre_gate * jax.nn.sigmoid(pre_gate) * pre_up).astype(jnp.bfloat16)
    return jnp.dot(hidden, down_weight, preferred_element_type=jnp.float32)


def backward_core(rows_in, grad_out, gate_weight, up_weight, down_weight):
    contract_rows = (((0,), (0,)), ((), ()))
    contract_cols = (((1,), (1,)), ((), ()))
    pre_gate = jnp.dot(rows_in, gate_weight, preferred_element_type=jnp.float32)
    pre_up = jnp.dot(rows_in, up_weight, preferred_element_type=jnp.float32)
    sigm_gate = jax.nn.sigmoid(pre_gate)
    swish = pre_gate * sigm_gate
    hidden = (swish * pre_up).astype(jnp.bfloat16)
    result = jnp.dot(hidden, down_weight, preferred_element_type=jnp.float32)
    grad_hidden = lax.dot_general(
        grad_out, down_weight, contract_cols, preferred_element_type=jnp.float32
    )
    grad_pre_up = (grad_hidden * swish).astype(jnp.bfloat16)
    grad_pre_gate = (
        grad_hidden * pre_up * sigm_gate * (1.0 + pre_gate * (1.0 - sigm_gate))
    ).astype(jnp.bfloat16)
    grad_down_w = lax.dot_general(
        hidden, grad_out, contract_rows, preferred_element_type=jnp.float32
    )
    grad_gate_w = lax.dot_general(
        rows_in, grad_pre_gate, contract_rows, preferred_element_type=jnp.float32
    )
    grad_up_w = lax.dot_general(
        rows_in, grad_pre_up, contract_rows, preferred_element_type=jnp.float32
    )
    grad_rows = lax.dot_general(
        grad_pre_gate, gate_weight, contract_cols, preferred_element_type=jnp.float32
    )
    grad_rows = grad_rows + lax.dot_general(
        grad_pre_up, up_weight, contract_cols, preferred_element_type=jnp.float32
    )
    return (result, grad_rows, grad_gate_w, grad_up_w, grad_down_w)


def shards(fwd_in, saved_in, out_grad, gain, router, w_gate, w_up, w_down, routes_fwd, routes_bwd):
    gain_row = gain[0]
    router_mat = router[0]
    gate_local = w_gate[0, 0]
    up_local = w_up[0, 0]
    down_local = w_down[0, 0]
    tokens = fwd_in.shape[1]
    model_width = fwd_in.shape[2]
    top_count = routes_fwd.shape[2]
    experts = router_mat.shape[1]
    capacity = max(3 * tokens * top_count // (2 * experts), 2)
    slot_count = experts * capacity
    slot_iota = jnp.arange(slot_count, dtype=jnp.int32)
    gate_full, up_full, down_full = (
        lax.all_gather(gate_local, "dp", axis=1, tiled=True),
        lax.all_gather(up_local, "dp", axis=1, tiled=True),
        lax.all_gather(down_local, "dp", axis=0, tiled=True),
    )
    as_float, inverse, normed = norm_rows(fwd_in[0], gain_row)
    gate_vals, selector = router_gates(normed, router_mat, routes_fwd[0])
    targets = route_slots(routes_fwd[0], experts, capacity)
    placing = slot_iota[:, None] == targets[None, :]
    by_token = placing.reshape(slot_count, tokens, top_count).any(axis=2).astype(jnp.bfloat16)
    packed = jnp.dot(by_token, normed, preferred_element_type=jnp.float32).astype(jnp.bfloat16)
    packed = packed.reshape(experts, capacity, model_width)
    expert_packed = lax.all_to_all(packed, "expert", split_axis=0, concat_axis=0, tiled=True)
    flat_rows = expert_packed.reshape(-1, model_width)
    combined = expert_result(flat_rows, gate_full, up_full, down_full)
    finished = combined.astype(jnp.bfloat16).reshape(expert_packed.shape)
    returned = lax.all_to_all(finished, "expert", split_axis=0, concat_axis=0, tiled=True)
    picked = returned.reshape(slot_count, model_width)[targets].reshape(
        tokens, top_count, model_width
    )
    mixed = (as_float + jnp.sum(gate_vals[:, :, None] * picked.astype(jnp.float32), axis=1)).astype(
        jnp.bfloat16
    )
    sent_fwd = shifted(mixed[None], "section", 1)
    cotangent = out_grad[0]
    cot_float = cotangent.astype(jnp.float32)
    saved_float, saved_inverse, saved_normed = norm_rows(saved_in[0], gain_row)
    saved_gates, saved_selector = router_gates(saved_normed, router_mat, routes_bwd[0])
    saved_targets = route_slots(routes_bwd[0], experts, capacity)
    saved_placing = slot_iota[:, None] == saved_targets[None, :]
    saved_by_token = (
        saved_placing.reshape(slot_count, tokens, top_count).any(axis=2).astype(jnp.bfloat16)
    )
    rows_packed = jnp.dot(saved_by_token, saved_normed, preferred_element_type=jnp.float32).astype(
        jnp.bfloat16
    )
    rows_packed = rows_packed.reshape(experts, capacity, model_width)
    scaled_cot = (saved_gates[:, :, None] * cot_float[:, None, :]).astype(jnp.bfloat16)
    scaled_cot = scaled_cot.reshape(tokens * top_count, model_width)
    grad_packed = jnp.dot(
        saved_placing.astype(jnp.bfloat16), scaled_cot, preferred_element_type=jnp.float32
    )
    grad_packed = grad_packed.astype(jnp.bfloat16).reshape(experts, capacity, model_width)
    rows_there, grads_there = (
        lax.all_to_all(rows_packed, "expert", split_axis=0, concat_axis=0, tiled=True),
        lax.all_to_all(grad_packed, "expert", split_axis=0, concat_axis=0, tiled=True),
    )
    result, grad_rows, grad_gate_w, grad_up_w, grad_down_w = backward_core(
        rows_there.reshape(-1, model_width),
        grads_there.reshape(-1, model_width),
        gate_full,
        up_full,
        down_full,
    )
    grad_gate_w, grad_up_w, grad_down_w = (
        lax.psum_scatter(
            grad_gate_w.astype(jnp.bfloat16), "dp", scatter_dimension=1, tiled=True
        ).astype(jnp.float32),
        lax.psum_scatter(
            grad_up_w.astype(jnp.bfloat16), "dp", scatter_dimension=1, tiled=True
        ).astype(jnp.float32),
        lax.psum_scatter(
            grad_down_w.astype(jnp.bfloat16), "dp", scatter_dimension=0, tiled=True
        ).astype(jnp.float32),
    )
    result, grad_rows, grad_gate_w, grad_up_w, grad_down_w = (
        result.astype(jnp.bfloat16),
        grad_rows.astype(jnp.bfloat16),
        grad_gate_w.astype(jnp.bfloat16),
        grad_up_w.astype(jnp.bfloat16),
        grad_down_w.astype(jnp.bfloat16),
    )
    result_back, rows_back = (
        lax.all_to_all(
            result.reshape(experts, capacity, model_width),
            "expert",
            split_axis=0,
            concat_axis=0,
            tiled=True,
        ),
        lax.all_to_all(
            grad_rows.reshape(experts, capacity, model_width),
            "expert",
            split_axis=0,
            concat_axis=0,
            tiled=True,
        ),
    )
    result_pick = result_back.reshape(slot_count, model_width)[saved_targets].reshape(
        tokens, top_count, model_width
    )
    gate_grad = jnp.sum(result_pick.astype(jnp.float32) * cot_float[:, None, :], axis=2)
    rows_pick = rows_back.reshape(slot_count, model_width)[saved_targets].reshape(
        tokens, top_count, model_width
    )
    dsel = gate_grad * saved_gates * (1.0 - saved_gates)
    dlogits = jnp.sum(saved_selector * dsel[:, :, None], axis=1).astype(jnp.bfloat16)
    router_part = lax.dot_general(
        saved_normed, dlogits, (((0,), (0,)), ((), ())), preferred_element_type=jnp.float32
    )
    dnormed = jnp.sum(rows_pick.astype(jnp.float32), axis=1)
    dnormed = dnormed + lax.dot_general(
        dlogits, router_mat, (((1,), (1,)), ((), ())), preferred_element_type=jnp.float32
    )
    scaled = dnormed * gain_row.astype(jnp.float32)
    gain_part = jnp.sum(dnormed * saved_float * saved_inverse, axis=0)
    in_grad = cot_float + saved_inverse * scaled
    in_grad = in_grad - saved_float * saved_inverse**3 * jnp.mean(
        scaled * saved_float, axis=-1, keepdims=True
    )
    sent_bwd = shifted(in_grad.astype(jnp.bfloat16)[None], "section", -1)
    router_total, gain_total = lax.psum((router_part, gain_part), ("expert", "dp"))
    return (
        sent_fwd,
        sent_bwd,
        grad_gate_w[None, None],
        grad_up_w[None, None],
        grad_down_w[None, None],
        router_total[None],
        gain_total[None],
    )


def solution(mesh):
    placed = (
        P("section", ("expert", "dp"), None),
        P("section", ("expert", "dp"), None),
        P("section", ("expert", "dp"), None),
        P("section", None),
        P("section", None, None),
        P("section", "expert", None, "dp"),
        P("section", "expert", None, "dp"),
        P("section", "expert", "dp", None),
        P("section", ("expert", "dp"), None),
        P("section", ("expert", "dp"), None),
    )
    return jax.shard_map(
        shards,
        mesh=mesh,
        in_specs=placed,
        out_specs=(
            P("section", ("expert", "dp"), None),
            P("section", ("expert", "dp"), None),
            P("section", "expert", None, "dp"),
            P("section", "expert", None, "dp"),
            P("section", "expert", "dp", None),
            P("section", None, None),
            P("section", None),
        ),
        check_vma=False,
    )
```

profile of v0, /device:TPU:1, one launch (start us, length us, event | category | flops | bytes accessed | tf_op | source)
XLA Modules:
  0.0 1067.0 jit_solution(17602125667431925862)
XLA Ops:
  13.3 11.9 %all-to-all-start.3 = ((bf16[32,12,2048]{2,1,0:T(8,128)(2,1)}), bf16[32,12,2048]{2,1,0:T(8,128)(2,1)S(1)}, u32[]{:S(2)}, u32[]{:S(2)}) async-start(bf16[32,12,2048]{2,1,0:T(8,128)(2,1)} %reshape.308), calls=%async_computation.3 | async-start | bytes 4194304 | tf_op jit(solution)/shard_map/all_to_all | solution.py:139
  26.0 47.7 %all-to-all-done.3 = bf16[32,12,2048]{2,1,0:T(8,128)(2,1)S(1)} async-done(((bf16[32,12,2048]{2,1,0:T(8,128)(2,1)}), bf16[32,12,2048]{2,1,0:T(8,128)(2,1)S(1)}, u32[]{:S(2)}, u32[]{:S(2)}) %all-to-all-start.3) | async-done | bytes 1572896 | tf_op jit(solution)/shard_map/all_to_all | solution.py:139
  75.0 5.6 fusion.14
  80.6 31.5 %all-gather.9.cloned.1.call-done = bf16[1,1,2048,704]{2,3,1,0:T(8,128)(2,1)} async-done(((bf16[1,1,2048,352]{2,3,1,0:T(8,128)(2,1)}), bf16[1,1,2048,704]{2,3,1,0:T(8,128)(2,1)}) %all-gather.9.cloned.1.call-update) | async-done | bytes 2883600 | tf_op jit(solution)/shard_map/all_gather | solution.py:97
  116.9 45.1 %all-gather.11.cloned.1.call-done = bf16[1,1,704,2048]{3,2,1,0:T(8,128)(2,1)} async-done(((bf16[1,1,352,2048]{3,2,1,0:T(8,128)(2,1)}), bf16[1,1,704,2048]{3,2,1,0:T(8,128)(2,1)}) %all-gather.11.cloned.1.call-update) | async-done | bytes 2883600 | tf_op jit(solution)/shard_map/all_gather | solution.py:98
  166.8 10.0 all-to-all-start.5
  183.8 41.4 %all-to-all-done.5 = bf16[32,12,2048]{2,1,0:T(8,128)(2,1)} async-done(((bf16[32,12,2048]{2,1,0:T(8,128)(2,1)}), bf16[32,12,2048]{2,1,0:T(8,128)(2,1)}, u32[]{:S(2)}, u32[]{:S(2)}) %all-to-all-start.5) | async-done | bytes 1572896 | tf_op jit(solution)/shard_map/all_to_all | solution.py:168
  240.2 6.6 all-to-all-start.2
  248.0 46.0 %all-to-all-done.2 = bf16[32,12,2048]{2,1,0:T(8,128)(2,1)S(1)} async-done(((bf16[32,12,2048]{2,1,0:T(8,128)(2,1)}), bf16[32,12,2048]{2,1,0:T(8,128)(2,1)S(1)}, u32[]{:S(2)}, u32[]{:S(2)}) %all-to-all-start.2) | async-done | bytes 1572896 | tf_op jit(solution)/shard_map/all_to_all | solution.py:140
  295.3 4.9 multiply_convert_fusion.3
  309.6 7.3 all-to-all-start
  321.9 41.5 %all-to-all-done = bf16[32,12,2048]{2,1,0:T(8,128)(2,1)S(1)} async-done(((bf16[32,12,2048]{2,1,0:T(8,128)(2,1)}), bf16[32,12,2048]{2,1,0:T(8,128)(2,1)S(1)}, u32[]{:S(2)}, u32[]{:S(2)}) %all-to-all-start) | async-done | bytes 1572896 | tf_op jit(solution)/shard_map/all_to_all | solution.py:107
  364.7 5.1 fusion.16
  369.8 6.8 fusion.18
  380.3 7.1 all-to-all-start.1
  398.0 35.4 %all-to-all-done.1 = bf16[32,12,2048]{2,1,0:T(8,128)(2,1)} async-done(((bf16[32,12,2048]{2,1,0:T(8,128)(2,1)}), bf16[32,12,2048]{2,1,0:T(8,128)(2,1)}, u32[]{:S(2)}, u32[]{:S(2)}) %all-to-all-start.1) | async-done | bytes 1572896 | tf_op jit(solution)/shard_map/all_to_all | solution.py:111
  433.4 7.7 all-to-all-start.4
  457.4 29.5 %all-to-all-done.4 = bf16[32,12,2048]{2,1,0:T(8,128)(2,1)} async-done(((bf16[32,12,2048]{2,1,0:T(8,128)(2,1)}), bf16[32,12,2048]{2,1,0:T(8,128)(2,1)}, u32[]{:S(2)}, u32[]{:S(2)}) %all-to-all-start.4) | async-done | bytes 1572896 | tf_op jit(solution)/shard_map/all_to_all | solution.py:175
  500.5 5.4 collective-permute-start.1
  505.8 158.4 %psum.15 = f32[1,2048]{1,0:T(1,128)} all-reduce(f32[1,2048]{1,0:T(1,128)S(1)} %bitcast.188), channel_id=1, replica_groups=mesh['section'=4,'expert'=32,'dp'=2] {'expert','dp'}, use_global_device_ids=true, to_apply=%region_22.23 | all-reduce | flops 2048 | bytes 16384 | tf_op jit(solution)/shard_map/psum | solution.py:206
  664.2 218.6 %all-reduce.2.cloned.1.call-done = f32[1,2048,32]{1,2,0:T(8,128)} async-done(((f32[1,2048,32]{1,2,0:T(8,128)}), f32[1,2048,32]{1,2,0:T(8,128)}) %all-reduce.2.cloned.1.call-update) | async-done | bytes 262160 | tf_op jit(solution)/shard_map/psum | solution.py:206
  882.8 75.3 %reduce-scatter.4.cloned.1.call-done = bf16[2048,352]{0,1:T(8,128)(2,1)} async-done(((bf16[2048,704]{0,1:T(8,128)(2,1)}), bf16[2048,352]{0,1:T(8,128)(2,1)}) %reduce-scatter.4.cloned.1.call-update) | async-done | bytes 1441808 | tf_op jit(solution)/shard_map/reduce_scatter | solution.py:150
  958.2 49.5 %reduce-scatter.6.cloned.1.call-done = bf16[2048,352]{0,1:T(8,128)(2,1)} async-done(((bf16[2048,704]{0,1:T(8,128)(2,1)}), bf16[2048,352]{0,1:T(8,128)(2,1)}) %reduce-scatter.6.cloned.1.call-update) | async-done | bytes 1441808 | tf_op jit(solution)/shard_map/reduce_scatter | solution.py:153
  1007.6 49.8 %reduce-scatter.8.cloned.1.call-done = bf16[352,2048]{1,0:T(8,128)(2,1)} async-done(((bf16[704,2048]{1,0:T(8,128)(2,1)}), bf16[352,2048]{1,0:T(8,128)(2,1)}) %reduce-scatter.8.cloned.1.call-update) | async-done | bytes 1441808 | tf_op jit(solution)/shard_map/reduce_scatter | solution.py:156
  (173 shorter events, 103.7 us)
Async XLA Ops:
  7.2 176.2 %copy-start = (bf16[1,2048,32]{1,2,0:T(8,128)(2,1)S(1)}, bf16[1,2048,32]{1,2,0:T(8,128)(2,1)}, u32[]{:S(2)}) copy-start(bf16[1,2048,32]{1,2,0:T(8,128)(2,1)} %param.14) | copy-start | bytes 393220
  7.2 67.8 %all-gather.7.cloned.1.call-start = ((), (), s32[]{:S(2)}) async-start(), calls=%async_computation.13 | async-start | bytes 4325376 | tf_op jit(solution)/shard_map/all_gather | solution.py:96
  7.9 104.2 %all-gather.9.cloned.1.call-start = ((), (), s32[]{:S(2)}) async-start(), calls=%async_computation.14 | async-start | bytes 4325376 | tf_op jit(solution)/shard_map/all_gather | solution.py:97
  11.2 235.7 %copy-start.21 = (f32[128]{0:T(128)}, f32[128]{0:T(128)S(1)}, u32[]{:S(2)}) copy-start(f32[128]{0:T(128)S(1)} %get-tuple-element.14) | copy-start | bytes 1540
  13.3 60.3 %all-to-all-start.3 = ((bf16[32,12,2048]{2,1,0:T(8,128)(2,1)}), bf16[32,12,2048]{2,1,0:T(8,128)(2,1)S(1)}, u32[]{:S(2)}, u32[]{:S(2)}) async-start(bf16[32,12,2048]{2,1,0:T(8,128)(2,1)} %reshape.308), calls=%async_computation.3 | async-start | bytes 4194304 | tf_op jit(solution)/shard_map/all_to_all | solution.py:139
  25.2 136.8 %all-gather.11.cloned.1.call-start = ((), (), s32[]{:S(2)}) async-start(), calls=%async_computation.15 | async-start | bytes 4325376 | tf_op jit(solution)/shard_map/all_gather | solution.py:98
  116.9 48.3 %copy-start.13 = (bf16[384,704]{0,1:T(8,128)(2,1)}, bf16[384,704]{0,1:T(8,128)(2,1)S(1)}, u32[]{:S(2)}) copy-start(bf16[384,704]{0,1:T(8,128)(2,1)S(1)} %get-tuple-element.15) | copy-start | bytes 1622020
  166.8 58.4 %all-to-all-start.5 = ((bf16[32,12,2048]{2,1,0:T(8,128)(2,1)}), bf16[32,12,2048]{2,1,0:T(8,128)(2,1)}, u32[]{:S(2)}, u32[]{:S(2)}) async-start(bf16[32,12,2048]{2,1,0:T(8,128)(2,1)} %reshape.312), calls=%async_computation.5 | async-start | bytes 4194304 | tf_op jit(solution)/shard_map/all_to_all | solution.py:168
  183.4 44.3 %copy-start.19 = (s32[1024]{0:T(1024)}, s32[1024]{0:T(1024)S(1)}, u32[]{:S(2)}) copy-start(s32[1024]{0:T(1024)S(1)} %pad_clamp_fusion) | copy-start | bytes 12292
  240.2 53.8 %all-to-all-start.2 = ((bf16[32,12,2048]{2,1,0:T(8,128)(2,1)}), bf16[32,12,2048]{2,1,0:T(8,128)(2,1)S(1)}, u32[]{:S(2)}, u32[]{:S(2)}) async-start(bf16[32,12,2048]{2,1,0:T(8,128)(2,1)} %reshape.306), calls=%async_computation.2 | async-start | bytes 4194304 | tf_op jit(solution)/shard_map/all_to_all | solution.py:140
  246.8 636.0 %all-reduce.2.cloned.1.call-start = ((), (), s32[]{:S(2)}) async-start(), calls=%async_computation.12 | async-start | bytes 524288 | tf_op jit(solution)/shard_map/psum | solution.py:206
  247.9 710.2 %reduce-scatter.4.cloned.1.call-start = ((), (), s32[]{:S(2)}) async-start(), calls=%async_computation.9 | async-start | bytes 4325376 | tf_op jit(solution)/shard_map/reduce_scatter | solution.py:150
  309.6 53.8 %all-to-all-start = ((bf16[32,12,2048]{2,1,0:T(8,128)(2,1)}), bf16[32,12,2048]{2,1,0:T(8,128)(2,1)S(1)}, u32[]{:S(2)}, u32[]{:S(2)}) async-start(bf16[32,12,2048]{2,1,0:T(8,128)(2,1)} %reshape.301), calls=%async_computation | async-start | bytes 4194304 | tf_op jit(solution)/shard_map/all_to_all | solution.py:107
  316.9 690.7 %reduce-scatter.6.cloned.1.call-start = ((), (), s32[]{:S(2)}) async-start(), calls=%async_computation.10 | async-start | bytes 4325376 | tf_op jit(solution)/shard_map/reduce_scatter | solution.py:153
  380.3 53.2 %all-to-all-start.1 = ((bf16[32,12,2048]{2,1,0:T(8,128)(2,1)}), bf16[32,12,2048]{2,1,0:T(8,128)(2,1)}, u32[]{:S(2)}, u32[]{:S(2)}) async-start(bf16[32,12,2048]{2,1,0:T(8,128)(2,1)} %reshape.303), calls=%async_computation.1 | async-start | bytes 4194304 | tf_op jit(solution)/shard_map/all_to_all | solution.py:111
  387.4 670.0 %reduce-scatter.8.cloned.1.call-start = ((), (), s32[]{:S(2)}) async-start(), calls=%async_computation.11 | async-start | bytes 4325376 | tf_op jit(solution)/shard_map/reduce_scatter | solution.py:156
  398.0 43.4 %copy-start.10 = (s32[1,128,2]{2,1,0:T(8,128)S(1)}, s32[1,128,2]{2,1,0:T(8,128)}, u32[]{:S(2)}) copy-start(s32[1,128,2]{2,1,0:T(8,128)} %copy-done.9) | copy-start | bytes 3076
  398.0 43.5 %copy-start.4 = (bf16[1,128,2048]{2,1,0:T(8,128)(2,1)S(1)}, bf16[1,128,2048]{2,1,0:T(8,128)(2,1)}, u32[]{:S(2)}) copy-start(bf16[1,128,2048]{2,1,0:T(8,128)(2,1)} %param.10) | copy-start | bytes 1572868
  398.0 43.5 %copy-start.27 = (f32[128]{0:T(128)S(1)}, f32[128]{0:T(128)}, u32[]{:S(2)}) copy-start(f32[128]{0:T(128)} %copy-done.26) | copy-start | bytes 1540
  398.0 44.0 %copy-start.18 = (s32[256]{0:T(256)S(1)}, s32[256]{0:T(256)}, u32[]{:S(2)}) copy-start(s32[256]{0:T(256)} %copy-done.17) | copy-start | bytes 3076
  433.4 53.5 %all-to-all-start.4 = ((bf16[32,12,2048]{2,1,0:T(8,128)(2,1)}), bf16[32,12,2048]{2,1,0:T(8,128)(2,1)}, u32[]{:S(2)}, u32[]{:S(2)}) async-start(bf16[32,12,2048]{2,1,0:T(8,128)(2,1)} %reshape.310), calls=%async_computation.4 | async-start | bytes 4194304 | tf_op jit(solution)/shard_map/all_to_all | solution.py:175
  453.4 52.4 %collective-permute-start = (bf16[1,128,2048]{2,1,0:T(8,128)(2,1)}, bf16[1,128,2048]{2,1,0:T(8,128)(2,1)S(1)}, u32[]{:S(2)}, u32[]{:S(2)}) collective-permute-start(bf16[1,128,2048]{2,1,0:T(8,128)(2,1)} %fusion.56), channel_id=1, source_target_pairs={{0,64},{64,128},{128,192},{192,0},{1,65},{65,129},{129,193},{193,1... | collective-permute-start | bytes 1572872 | tf_op jit(solution)/shard_map/ppermute | solution.py:12
  500.5 163.8 %collective-permute-start.1 = (bf16[1,128,2048]{2,1,0:T(8,128)(2,1)S(1)}, bf16[1,128,2048]{2,1,0:T(8,128)(2,1)S(1)}, u32[]{:S(2)}, u32[]{:S(2)}) collective-permute-start(bf16[1,128,2048]{2,1,0:T(8,128)(2,1)S(1)} %fusion.68), channel_id=1, source_target_pairs={{0,192},{64,0},{128,64},{192,128},{1,193},{65,1},{129,65},{193,129... | collective-permute-start | bytes 1572872 | tf_op jit(solution)/shard_map/ppermute | solution.py:12
  882.8 176.1 %copy-start.16 = (f32[1,2048,32]{1,2,0:T(8,128)S(1)}, f32[1,2048,32]{1,2,0:T(8,128)}, u32[]{:S(2)}) copy-start(f32[1,2048,32]{1,2,0:T(8,128)} %all-reduce.2.cloned.1.call-done) | copy-start | bytes 786436
  (20 other events, 149.1 us)
Sparse Core Ops, SparseCore 0:
  9.8 52.3 all-gather.6
  64.1 48.0 all-gather.8
  113.9 48.0 all-gather.10
  250.5 632.2 all-reduce.1
  885.9 72.2 reduce-scatter.3
  961.1 46.4 reduce-scatter.5
  1010.9 46.4 reduce-scatter.7
where the time goes:
time: 1070 us
  waiting for transfers between devices  713 us (67%)
  blocking collectives  158 us (15%)
  starting transfers between devices  60.3 us (6%)
  matrix products  54.5 us (5%)
  local copies, waits for them, and re-layouts  51.2 us (5%)
  between operations  15.2 us (1%)
  other arithmetic  13.9 us (1%)
    psum x1, waiting for transfers between devices, shards(): lax.psum((router_part, gain_part), ('expert', 'dp'))  219 us
    psum x1, blocking collectives, shards(): lax.psum((router_part, gain_part), ('expert', 'dp'))  158 us
    reduce_scatter x1, waiting for transfers between devices, shards(): lax.psum_scatter(grad_gate_w.astype(jnp.bfloat16), 'dp', scatter_dimensio...  75.3 us
    reduce_scatter x1, waiting for transfers between devices, shards(): lax.psum_scatter(grad_down_w.astype(jnp.bfloat16), 'dp', scatter_dimensio...  49.8 us
    reduce_scatter x1, waiting for transfers between devices, shards(): lax.psum_scatter(grad_up_w.astype(jnp.bfloat16), 'dp', scatter_dimension=...  49.5 us
    all_to_all x1, waiting for transfers between devices, shards(): lax.all_to_all(rows_packed, 'expert', split_axis=0, concat_axis=0, tiled=...  47.7 us
    all_to_all x1, waiting for transfers between devices, shards(): lax.all_to_all(grad_packed, 'expert', split_axis=0, concat_axis=0, tiled=...  46 us
    all_gather x1, waiting for transfers between devices, shards(): lax.all_gather(down_local, 'dp', axis=0, tiled=True)  45.1 us
  transfers between devices with their start and end apart: 15, of which 12 were waited for; matrix products, arithmetic and copies ran while one was open for 9% of the time, Pallas kernels for 0%

commit v1 on v0

v1 whole, which is shorter than its diff:
```python
import jax
import jax.numpy as jnp
from jax import lax
from jax.experimental import pallas as pl
from jax.experimental.pallas import tpu as pltpu
from jax.sharding import PartitionSpec as P

EPS = 1e-06
MESH = pl.DeviceIdType.MESH
EXPERTS = 32
CAP = 12
GROUPS = 3
QUARTS = 4
SLAB = 512
BLOCK = 16
F32 = jnp.float32
BF16 = jnp.bfloat16


def peer_of(me, step):
    return lax.rem(me // 4 + step // 4, 8) * 4 + lax.rem(me + step, 4)


def remote(src, dst, send_sem, recv_sem, device):
    return pltpu.make_async_remote_copy(
        src_ref=src,
        dst_ref=dst,
        send_sem=send_sem,
        recv_sem=recv_sem,
        device_id=device,
        device_id_type=MESH,
    )


def dot(left, right, left_dim=1, right_dim=0):
    return lax.dot_general(
        left, right, (((left_dim,), (right_dim,)), ((), ())), preferred_element_type=F32
    )


def norm_rows(inputs, gain_row):
    as_float = inputs.astype(F32)
    inverse = lax.rsqrt(jnp.mean(as_float * as_float, axis=-1, keepdims=True) + EPS)
    normed = (as_float * inverse * gain_row).astype(BF16)
    return as_float, inverse, normed


def place(places, routes):
    tokens = routes.shape[0]
    lanes = lax.broadcasted_iota(jnp.int32, (tokens, EXPERTS), 1)
    named = (routes[:, 0:1] == lanes) | (routes[:, 1:2] == lanes)
    earlier = (
        lax.broadcasted_iota(jnp.int32, (tokens, tokens), 1)
        < lax.broadcasted_iota(jnp.int32, (tokens, tokens), 0)
    ).astype(F32)
    before = dot(earlier.astype(BF16), named.astype(F32).astype(BF16))
    slots = jnp.where(named, before, -1.0).astype(BF16)
    rows = EXPERTS * BLOCK
    row = lax.broadcasted_iota(jnp.int32, (rows, EXPERTS), 0)
    repeat = (row >> 4) == lax.broadcasted_iota(jnp.int32, (rows, EXPERTS), 1)
    wide = dot(repeat.astype(F32).astype(BF16), slots, 1, 1)
    row = lax.broadcasted_iota(jnp.int32, (rows, tokens), 0)
    quarter = (row >> 2) & 3
    slot = (row & 3).astype(F32)
    for group in range(GROUPS):
        hit = jnp.where(wide == slot + 4.0 * group, 1.0, 0.0)
        for q in range(QUARTS):
            places[group, :, q * tokens : (q + 1) * tokens] = jnp.where(
                quarter == q, hit, 0.0
            ).astype(BF16)


def pack(places, rows, packed):
    stacked = jnp.concatenate(
        [rows[:, q * SLAB : (q + 1) * SLAB] for q in range(QUARTS)], axis=0
    )
    for group in range(GROUPS):
        packed[:, group * SLAB : (group + 1) * SLAB] = dot(places[group], stacked).astype(BF16)


def combine(places, returned):
    total = dot(places[0], returned[:, 0:SLAB], 0, 0)
    for group in range(1, GROUPS):
        total = total + dot(places[group], returned[:, group * SLAB : (group + 1) * SLAB], 0, 0)
    tokens = total.shape[0] // QUARTS
    return jnp.concatenate(
        [total[q * tokens : (q + 1) * tokens] for q in range(QUARTS)], axis=1
    )


def shuffle():
    row = lax.broadcasted_iota(jnp.int32, (128, 128), 0)
    col = lax.broadcasted_iota(jnp.int32, (128, 128), 1)
    wanted = (((row >> 2) & 7) << 4) + ((row >> 5) << 2) + (row & 3)
    return jnp.where(col == wanted, 1.0, 0.0).astype(BF16)


def unpack(received, rows):
    order = shuffle()
    for at in range(4):
        part = dot(order, received[at * 128 : (at + 1) * 128, :]).astype(BF16)
        for group in range(GROUPS):
            for q in range(QUARTS):
                rows[
                    group * 128 + at * 32 : group * 128 + (at + 1) * 32,
                    q * SLAB : (q + 1) * SLAB,
                ] = part[q * 32 : (q + 1) * 32, group * SLAB : (group + 1) * SLAB]


def repack(rows, packed):
    order = shuffle()
    for at in range(4):
        for group in range(GROUPS):
            part = jnp.concatenate(
                [
                    rows[
                        group * 128 + at * 32 : group * 128 + (at + 1) * 32,
                        q * SLAB : (q + 1) * SLAB,
                    ]
                    for q in range(QUARTS)
                ],
                axis=0,
            ).astype(BF16)
            packed[at * 128 : (at + 1) * 128, group * SLAB : (group + 1) * SLAB] = dot(
                order, part, 0, 0
            ).astype(BF16)


def slabs():
    def over(body):
        @pl.loop(0, QUARTS)
        def _(q):
            body(pl.ds(pl.multiple_of(q * SLAB, SLAB), SLAB))

    return over


def backward_half(rows, scaled, weights, hidden, grad_gate, grad_up, grad_rows, add):
    gate, up, down = weights
    pre_gate, pre_up = dot(rows[...], gate[...], 1, 1), dot(rows[...], up[...], 1, 1)
    grad_hidden = dot(scaled[...], down[...], 1, 1)
    sigm = jax.nn.sigmoid(pre_gate)
    swish = pre_gate * sigm
    hidden[...] = (swish * pre_up).astype(BF16)
    share = jnp.sum(hidden[...].astype(F32) * grad_hidden, axis=1, keepdims=True)
    grad_up[...] = (grad_hidden * swish).astype(BF16)
    grad_gate[...] = (
        grad_hidden * pre_up * sigm * (1.0 + pre_gate * (1.0 - sigm))
    ).astype(BF16)

    @slabs()
    def _(cols):
        part = dot(grad_gate[...], gate[:, cols]) + dot(grad_up[...], up[:, cols])
        grad_rows[:, cols] = grad_rows[:, cols] + part if add else part

    return share


def weight_grad(left, right, target, addend):
    turned = left[...].T

    @slabs()
    def _(cols):
        part = dot(turned, right[:, cols])
        if addend is not None:
            part = part + addend[:, cols].astype(F32)
        target[:, cols] = part.astype(BF16)


def relay_kernel(*refs):
    (
        fwd_in,
        saved_in,
        out_grad,
        gain,
        router,
        w_gate,
        w_up,
        w_down,
        routes_fwd,
        routes_bwd,
        sent_fwd,
        sent_bwd,
        total_gate,
        total_up,
        total_down,
        router_total,
        gain_total,
        places_fwd,
        places_bwd,
        out_blocks,
        in_blocks,
        rows,
        scaled,
        rows_fwd,
        far,
        hidden,
        grad_gate,
        grad_up,
        fwd_hidden,
        grad_rows,
        far_grads,
        there_grads,
        back_out,
        back_in,
        shift_out,
        vec,
        vec_other,
        vec_sum,
        vecs,
        out_send,
        out_recv,
        back_send,
        back_recv,
        local,
        far_send,
        far_recv,
        grad_send,
        grad_recv,
        shift_send,
        shift_recv,
        pair_sems,
        vec_send,
        vec_recv,
    ) = refs
    me = lax.axis_index("expert")
    other = {"dp": 1 - lax.axis_index("dp")}
    section = lax.axis_index("section")
    after = {"section": lax.rem(section + 1, 4)}
    ahead = {"section": lax.rem(section + 3, 4)}
    own = (w_gate, w_up, w_down)
    fars = tuple(far.at[at] for at in range(3))

    barrier = pltpu.get_barrier_semaphore()

    @pl.loop(1, EXPERTS)
    def _(step):
        pl.semaphore_signal(
            barrier, inc=1, device_id={"expert": peer_of(me, step)}, device_id_type=MESH
        )

    for device in (other, after, ahead):
        pl.semaphore_signal(barrier, inc=1, device_id=device, device_id_type=MESH)

    def block(of):
        return pl.ds(pl.multiple_of(of * BLOCK, BLOCK), BLOCK)

    def each(sources, targets, send, recv, act):
        @pl.loop(1, EXPERTS)
        def _(step):
            peer = peer_of(me, step)
            act(
                remote(
                    sources.at[block(peer)],
                    targets.at[block(me)],
                    send.at[step],
                    recv.at[step],
                    {"expert": peer},
                )
            )

    def own_block(sources, targets, sem):
        return pltpu.make_async_copy(sources.at[block(me)], targets.at[block(me)], sem)

    def issue(sources, targets, send, recv, sem):
        own_block(sources, targets, sem).start()
        each(sources, targets, send, recv, lambda copy: copy.start())

    def arrive(sources, targets, send, recv, sem):
        own_block(sources, targets, sem).wait()
        each(sources, targets, send, recv, lambda copy: copy.wait())

    def outward(at):
        return (
            out_blocks.at[at], in_blocks.at[at], out_send.at[at], out_recv.at[at], local.at[at],
        )

    def homeward(at):
        return (
            back_out.at[at], back_in.at[at], back_send.at[at], back_recv.at[at], local.at[3 + at],
        )

    gain_row = gain[...].astype(F32)
    place(places_bwd, routes_bwd[...])
    normed = norm_rows(saved_in[...], gain_row)[2]
    pack(places_bwd, normed, out_blocks.at[0])

    pl.semaphore_wait(barrier, EXPERTS + 2)
    issue(*outward(0))
    weight_moves = [
        remote(own[at], fars[at], far_send.at[at], far_recv.at[at], other) for at in range(3)
    ]
    for move in weight_moves:
        move.start()
    pack(places_bwd, out_grad[...], out_blocks.at[1])
    issue(*outward(1))
    place(places_fwd, routes_fwd[...])
    normed = norm_rows(fwd_in[...], gain_row)[2]
    pack(places_fwd, normed, out_blocks.at[2])

    lanes = lax.broadcasted_iota(jnp.int32, (rows.shape[0], EXPERTS), 1)

    def gates(of):
        logits = dot(of[...], router[...], 1, 1)
        return jax.nn.sigmoid(jnp.sum(jnp.where(lanes == me, logits, 0.0), axis=1, keepdims=True))

    arrive(*outward(0))
    issue(*outward(2))
    unpack(in_blocks.at[0], rows)
    gate_bwd = gates(rows)
    arrive(*outward(1))
    unpack(in_blocks.at[1], scaled)

    @slabs()
    def _(cols):
        scaled[:, cols] = (gate_bwd * scaled[:, cols].astype(F32)).astype(BF16)

    def half(weights, at, add):
        return backward_half(
            rows, scaled, weights, hidden.at[at], grad_gate.at[at], grad_up.at[at], grad_rows, add
        )

    share = half(own, 0, False)
    for move in weight_moves:
        move.wait()
    share = share + half(fars, 1, True)
    grad_moves = [
        remote(
            far_grads.at[at], there_grads.at[at], grad_send.at[at], grad_recv.at[at], other
        )
        for at in range(3)
    ]

    factors = ((grad_gate, rows), (grad_up, rows), (hidden, scaled))
    for at, (left, right) in enumerate(factors):
        weight_grad(left.at[1], right, far_grads.at[at], None)
        grad_moves[at].start()

    dlogit = (share * (1.0 - gate_bwd)).astype(BF16).astype(F32)
    row = lax.broadcasted_iota(jnp.int32, router.shape, 0)
    mine = jnp.sum(jnp.where(row == me, router[...].astype(F32), 0.0), axis=0, keepdims=True)
    for q in range(QUARTS):
        cols = slice(q * SLAB, (q + 1) * SLAB)
        part = grad_rows[:, cols] + dlogit * mine[:, cols]
        grad_rows[:, cols] = part
        rows_float = rows[:, cols].astype(F32)
        router_column = jnp.sum(rows_float * dlogit, axis=0, keepdims=True)
        gain_part = jnp.sum(rows_float * part, axis=0, keepdims=True) / gain_row[:, cols]
        for at in range(4):
            vec[q * 4 + at : q * 4 + at + 1, :] = router_column[:, at * 128 : (at + 1) * 128]
            vec[16 + q * 4 + at : 17 + q * 4 + at, :] = gain_part[:, at * 128 : (at + 1) * 128]
    repack(grad_rows, back_out.at[0])
    issue(*homeward(0))
    pair = remote(vec, vec_other, pair_sems.at[0], pair_sems.at[1], other)
    pair.start()

    arrive(*outward(2))
    unpack(in_blocks.at[2], rows_fwd)
    gate_fwd = gates(rows_fwd)
    for at, (gate, up, down) in enumerate((own, fars)):
        pre_gate, pre_up = dot(rows_fwd[...], gate[...], 1, 1), dot(rows_fwd[...], up[...], 1, 1)
        fwd_hidden[...] = (pre_gate * jax.nn.sigmoid(pre_gate) * pre_up).astype(BF16)

        @slabs()
        def _(cols):
            part = gate_fwd * dot(fwd_hidden[...], down[:, cols])
            grad_rows[:, cols] = grad_rows[:, cols] + part if at else part

    repack(grad_rows, back_out.at[1])
    issue(*homeward(1))

    pair.wait()
    vec_sum[...] = vec[...] + vec_other[...]
    vecs[me] = vec_sum[...]

    def share_vec(act):
        @pl.loop(1, EXPERTS)
        def _(step):
            act(
                remote(
                    vec_sum,
                    vecs.at[me],
                    vec_send.at[step],
                    vec_recv.at[step],
                    {"expert": peer_of(me, step)},
                )
            )

    share_vec(lambda copy: copy.start())

    arrive(*homeward(0))
    dnormed = combine(places_bwd, back_in.at[0])
    x_bwd, inverse, _ = norm_rows(saved_in[...], gain_row)
    scaled_grad = dnormed * gain_row
    mean = jnp.mean(scaled_grad * x_bwd, axis=-1, keepdims=True)
    in_grad = out_grad[...].astype(F32) + inverse * scaled_grad - x_bwd * inverse**3 * mean
    shift_out[0] = in_grad.astype(BF16)
    shift_bwd = remote(shift_out.at[0], sent_bwd, shift_send.at[0], shift_recv.at[0], ahead)
    shift_bwd.start()

    arrive(*homeward(1))
    mixed = fwd_in[...].astype(F32) + combine(places_fwd, back_in.at[1])
    shift_out[1] = mixed.astype(BF16)
    shift_fwd = remote(shift_out.at[1], sent_fwd, shift_send.at[1], shift_recv.at[1], after)
    shift_fwd.start()

    share_vec(lambda copy: copy.wait())
    gain_total[...] = jnp.sum(vecs[:, 16:32, :], axis=0)
    for at in range(16):
        router_total[:, at * 128 : (at + 1) * 128] = vecs[:, at, :]

    totals = (total_gate, total_up, total_down)
    for at, (left, right) in enumerate(factors):
        grad_moves[at].wait()
        weight_grad(left.at[0], right, totals[at], there_grads.at[at])
    shift_bwd.wait()
    shift_fwd.wait()


def relay(*operands):
    fwd_in, router, w_down = operands[0], operands[4], operands[7]
    tokens, width = fwd_in.shape
    half = w_down.shape[0]
    packed = (EXPERTS * BLOCK, GROUPS * SLAB)
    pairs = EXPERTS * CAP
    vmem = pl.BlockSpec(memory_space=pltpu.VMEM)
    dma = pltpu.SemaphoreType.DMA
    out_shape = [
        jax.ShapeDtypeStruct((tokens, width), BF16),
        jax.ShapeDtypeStruct((tokens, width), BF16),
        jax.ShapeDtypeStruct((half, width), BF16),
        jax.ShapeDtypeStruct((half, width), BF16),
        jax.ShapeDtypeStruct((half, width), BF16),
        jax.ShapeDtypeStruct((EXPERTS, width), F32),
        jax.ShapeDtypeStruct((16, 128), F32),
    ]
    scratch = [
        pltpu.VMEM((GROUPS, packed[0], QUARTS * tokens), BF16),
        pltpu.VMEM((GROUPS, packed[0], QUARTS * tokens), BF16),
        pltpu.VMEM((3,) + packed, BF16),
        pltpu.VMEM((3,) + packed, BF16),
        pltpu.VMEM((pairs, width), BF16),
        pltpu.VMEM((pairs, width), BF16),
        pltpu.VMEM((pairs, width), BF16),
        pltpu.VMEM((3, half, width), BF16),
        pltpu.VMEM((2, pairs, half), BF16),
        pltpu.VMEM((2, pairs, half), BF16),
        pltpu.VMEM((2, pairs, half), BF16),
        pltpu.VMEM((pairs, half), BF16),
        pltpu.VMEM((pairs, width), F32),
        pltpu.VMEM((3, half, width), BF16),
        pltpu.VMEM((3, half, width), BF16),
        pltpu.VMEM((2,) + packed, BF16),
        pltpu.VMEM((2,) + packed, BF16),
        pltpu.VMEM((2, tokens, width), BF16),
        pltpu.VMEM((32, 128), F32),
        pltpu.VMEM((32, 128), F32),
        pltpu.VMEM((32, 128), F32),
        pltpu.VMEM((EXPERTS, 32, 128), F32),
        dma((3, EXPERTS)),
        dma((3, EXPERTS)),
        dma((2, EXPERTS)),
        dma((2, EXPERTS)),
        dma((5,)),
        dma((3,)),
        dma((3,)),
        dma((3,)),
        dma((3,)),
        dma((2,)),
        dma((2,)),
        dma((2,)),
        dma((EXPERTS,)),
        dma((EXPERTS,)),
    ]
    return pl.pallas_call(
        relay_kernel,
        out_shape=out_shape,
        in_specs=[vmem] * len(operands),
        out_specs=[vmem] * len(out_shape),
        scratch_shapes=scratch,
        compiler_params=pltpu.CompilerParams(
            collective_id=0, has_side_effects=True, vmem_limit_bytes=63 << 20
        ),
        name="relay",
    )(*operands)


def shards(fwd_in, saved_in, out_grad, gain, router, w_gate, w_up, w_down, routes_fwd, routes_bwd):
    sent_fwd, sent_bwd, total_gate, total_up, total_down, router_total, gain_total = relay(
        fwd_in[0],
        saved_in[0],
        out_grad[0],
        gain,
        router[0].T,
        w_gate[0, 0].T,
        w_up[0, 0].T,
        w_down[0, 0],
        routes_fwd[0],
        routes_bwd[0],
    )
    return (
        sent_fwd[None],
        sent_bwd[None],
        total_gate.T[None, None],
        total_up.T[None, None],
        total_down[None, None],
        router_total.T[None],
        gain_total.reshape(1, -1),
    )


def solution(mesh):
    tokens = P("section", ("expert", "dp"), None)
    wide = P("section", "expert", None, "dp")
    deep = P("section", "expert", "dp", None)
    gain, router = P("section", None), P("section", None, None)
    return jax.shard_map(
        shards,
        mesh=mesh,
        in_specs=(tokens, tokens, tokens, gain, router, wide, wide, deep, tokens, tokens),
        out_specs=(tokens, tokens, wide, wide, deep, router, gain),
        check_vma=False,
    )
```

time: 1070 us -> 246 us (0.23)
  waiting for transfers between devices: 713 us -> 0 us
  Pallas kernels: 0 us -> 232 us
  blocking collectives: 158 us -> 0 us
  starting transfers between devices: 60.3 us -> 0 us
  matrix products: 54.5 us -> 0 us
  local copies, waits for them, and re-layouts: 51.2 us -> 12.9 us
  between operations: 15.2 us -> 0.66 us
  other arithmetic: 13.9 us -> 0 us
    all_to_all x6 -> x0, waiting for transfers between devices: 242 us -> none  [the longest x1 47.7 us: shards(): lax.all_to_all(rows_packed, 'expert', split_axis=0, concat_axis=0, tiled=...]
    pallas_call x0 -> x1, Pallas kernels: none -> 232 us  [relay(): pl.pallas_call(relay_kernel, out_shape=out_shape, in_specs=[vmem] * len(o...]
    psum x1 -> x0, waiting for transfers between devices: 219 us -> none  [shards(): lax.psum((router_part, gain_part), ('expert', 'dp'))]
    reduce_scatter x3 -> x0, waiting for transfers between devices: 175 us -> none  [the longest x1 75.3 us: shards(): lax.psum_scatter(grad_gate_w.astype(jnp.bfloat16), 'dp', scatter_dimensio...]
    psum x1 -> x0, blocking collectives: 158 us -> none  [shards(): lax.psum((router_part, gain_part), ('expert', 'dp'))]
    all_gather x3 -> x0, waiting for transfers between devices: 76.6 us -> none  [the longest x1 45.1 us: shards(): lax.all_gather(down_local, 'dp', axis=0, tiled=True)]
    dot_general x18 -> x0, matrix products: 54.5 us -> none  [the longest x1 6.84 us: expert_result(): return jnp.dot(hidden, down_weight, preferred_element_type=jnp.float32)]
    all_to_all x6 -> x0, starting transfers between devices: 50.5 us -> none  [the longest x1 11.9 us: shards(): lax.all_to_all(rows_packed, 'expert', split_axis=0, concat_axis=0, tiled=...]
  transfers between devices with their start and end apart: 15 -> 0, of which waited for: 12 -> 0; matrix products, arithmetic and copies ran while one was open for 9% -> 0% of each run, Pallas kernels for 0% -> 0%
where the time goes in v1:
time: 246 us
  Pallas kernels  232 us (94%)
  local copies, waits for them, and re-layouts  12.9 us (5%)
    pallas_call x1, Pallas kernels, relay(): pl.pallas_call(relay_kernel, out_shape=out_shape, in_specs=[vmem] * len(o...  232 us
    unnamed x19, local copies, waits for them, and re-layouts  12.9 us

profile of v1, /device:TPU:1, one launch (start us, length us, event | category | flops | bytes accessed | tf_op | source)
XLA Modules:
  0.0 245.8 jit_solution(9012072837671951486)
XLA Ops:
  0.6 1.4 copy.17
  2.0 1.4 copy.18
  3.5 232.2 %relay.1 = (bf16[128,2048]{1,0:T(8,128)(2,1)}, bf16[128,2048]{1,0:T(8,128)(2,1)}, bf16[352,2048]{1,0:T(8,128)(2,1)}, bf16[352,2048]{1,0:T(8,128)(2,1)}, bf16[352...) custom-call(bf16[128,2048]{1,0:T(8,128)(2,1)} %bitcast.34, bf16[128,2048]{1,0:T(8,128)(2,1)} %bitcast.35, ...), custom_call_target="tpu_custom_call" | custom-call | tf_op jit(solution)/shard_map/relay/pallas_call | solution.py:475
  235.7 0.0 copy-start.2
  235.7 2.0 copy.26
  237.7 1.9 copy.27
  239.6 0.0 copy-done.2
  239.6 0.0 copy-start.1
  239.6 1.1 copy.28
  240.7 0.8 copy-done.1
  241.5 0.0 copy-start
  241.5 1.1 copy.29
  242.6 0.8 copy-done
  243.3 0.0 copy-start.3
  243.3 0.0 copy-start.4
  243.4 1.1 copy.30
  244.4 0.0 copy-done.3
  244.5 0.7 copy.31
  245.2 0.0 copy-done.4
  245.2 0.6 copy.32
Async XLA Ops:
  235.7 3.9 %copy-start.2 = (bf16[352,2048]{1,0:T(8,128)(2,1)S(1)}, bf16[352,2048]{1,0:T(8,128)(2,1)}, u32[]{:S(2)}) copy-start(bf16[352,2048]{1,0:T(8,128)(2,1)} %get-tuple-element.16) | copy-start | bytes 4325380
  239.6 1.9 copy-start.1
  241.5 1.9 copy-start
  243.3 1.1 copy-start.3
  243.3 1.8 copy-start.4

commit v2 on v1

--- a/solution.py
+++ b/solution.py
@@ -13,6 +13,7 @@
 QUARTS = 4
 SLAB = 512
 BLOCK = 16
+FIRST = 256
 F32 = jnp.float32
 BF16 = jnp.bfloat16
 
@@ -46,19 +47,19 @@
 
 
 def place(places, routes):
-    tokens = routes.shape[0]
-    lanes = lax.broadcasted_iota(jnp.int32, (tokens, EXPERTS), 1)
-    named = (routes[:, 0:1] == lanes) | (routes[:, 1:2] == lanes)
+    tokens = routes.shape[1]
+    experts = lax.broadcasted_iota(jnp.int32, (EXPERTS, tokens), 0)
+    named = (routes[0:1, :] == experts) | (routes[1:2, :] == experts)
     earlier = (
-        lax.broadcasted_iota(jnp.int32, (tokens, tokens), 1)
-        < lax.broadcasted_iota(jnp.int32, (tokens, tokens), 0)
+        lax.broadcasted_iota(jnp.int32, (tokens, tokens), 0)
+        < lax.broadcasted_iota(jnp.int32, (tokens, tokens), 1)
     ).astype(F32)
-    before = dot(earlier.astype(BF16), named.astype(F32).astype(BF16))
+    before = dot(named.astype(F32).astype(BF16), earlier.astype(BF16))
     slots = jnp.where(named, before, -1.0).astype(BF16)
     rows = EXPERTS * BLOCK
     row = lax.broadcasted_iota(jnp.int32, (rows, EXPERTS), 0)
     repeat = (row >> 4) == lax.broadcasted_iota(jnp.int32, (rows, EXPERTS), 1)
-    wide = dot(repeat.astype(F32).astype(BF16), slots, 1, 1)
+    wide = dot(repeat.astype(F32).astype(BF16), slots)
     row = lax.broadcasted_iota(jnp.int32, (rows, tokens), 0)
     quarter = (row >> 2) & 3
     slot = (row & 3).astype(F32)
@@ -135,25 +136,31 @@
     return over
 
 
-def backward_half(rows, scaled, weights, hidden, grad_gate, grad_up, grad_rows, add):
-    gate, up, down = weights
-    pre_gate, pre_up = dot(rows[...], gate[...], 1, 1), dot(rows[...], up[...], 1, 1)
-    grad_hidden = dot(scaled[...], down[...], 1, 1)
+def pre_activate(rows, piece):
+    piece.pre_gate[...] = dot(rows[...], piece.gate[...], 1, 1)
+    piece.pre_up[...] = dot(rows[...], piece.up[...], 1, 1)
+
+
+def backward_piece(scaled, piece):
+    grad_hidden = dot(scaled[...], piece.down[...], 1, 1)
+    pre_gate, pre_up = piece.pre_gate[...], piece.pre_up[...]
     sigm = jax.nn.sigmoid(pre_gate)
     swish = pre_gate * sigm
-    hidden[...] = (swish * pre_up).astype(BF16)
-    share = jnp.sum(hidden[...].astype(F32) * grad_hidden, axis=1, keepdims=True)
-    grad_up[...] = (grad_hidden * swish).astype(BF16)
-    grad_gate[...] = (
+    hidden = (swish * pre_up).astype(BF16)
+    piece.hidden[...] = hidden
+    piece.grad_up[...] = (grad_hidden * swish).astype(BF16)
+    piece.grad_gate[...] = (
         grad_hidden * pre_up * sigm * (1.0 + pre_gate * (1.0 - sigm))
     ).astype(BF16)
-
+    return jnp.sum(hidden.astype(F32) * grad_hidden, axis=1, keepdims=True)
+
+
+def row_grads(piece, grad_rows, add):
     @slabs()
     def _(cols):
-        part = dot(grad_gate[...], gate[:, cols]) + dot(grad_up[...], up[:, cols])
+        part = dot(piece.grad_gate[...], piece.gate[:, cols])
+        part = part + dot(piece.grad_up[...], piece.up[:, cols])
         grad_rows[:, cols] = grad_rows[:, cols] + part if add else part
-
-    return share
 
 
 def weight_grad(left, right, target, addend):
@@ -164,72 +171,45 @@
         part = dot(turned, right[:, cols])
         if addend is not None:
             part = part + addend[:, cols].astype(F32)
-        target[:, cols] = part.astype(BF16)
+        target[:, cols] = part.astype(target.dtype)
+
+
+class Piece:
+    def __init__(self, weights, kept):
+        self.gate, self.up, self.down = weights
+        self.pre_gate, self.pre_up, self.hidden, self.grad_gate, self.grad_up = kept
 
 
 def relay_kernel(*refs):
-    (
-        fwd_in,
-        saved_in,
-        out_grad,
-        gain,
-        router,
-        w_gate,
-        w_up,
-        w_down,
-        routes_fwd,
-        routes_bwd,
-        sent_fwd,
-        sent_bwd,
-        total_gate,
-        total_up,
-        total_down,
-        router_total,
-        gain_total,
-        places_fwd,
-        places_bwd,
-        out_blocks,
-        in_blocks,
-        rows,
-        scaled,
-        rows_fwd,
-        far,
-        hidden,
-        grad_gate,
-        grad_up,
-        fwd_hidden,
-        grad_rows,
-        far_grads,
-        there_grads,
-        back_out,
-        back_in,
-        shift_out,
-        vec,
-        vec_other,
-        vec_sum,
-        vecs,
-        out_send,
-        out_recv,
-        back_send,
-        back_recv,
-        local,
-        far_send,
-        far_recv,
-        grad_send,
-        grad_recv,
-        shift_send,
-        shift_recv,
-        pair_sems,
-        vec_send,
-        vec_recv,
-    ) = refs
+    refs = list(refs)
+
+    def take(count):
+        taken = refs[:count]
+        del refs[:count]
+        return taken
+
+    fwd_in, saved_in, out_grad, gain, router = take(5)
+    own_hbm = take(3)
+    routes_fwd, routes_bwd = take(2)
+    sent_fwd, sent_bwd = take(2)
+    totals = take(3)
+    router_total, gain_total = take(2)
+    places_fwd, places_bwd, out_blocks, in_blocks, rows, scaled, rows_fwd, near, far = take(9)
+    kept_near, kept_first, kept_last = take(5), take(5), take(5)
+    fwd_hidden, grad_rows, far_grads, there_grads, back_out, back_in, shift_out = take(7)
+    near_last = take(1)[0]
+    vec, vec_other, vec_sum, vecs = take(4)
+    out_send, out_recv, back_send, back_recv, local = take(5)
+    near_sems, far_send, far_recv, grad_send, grad_recv, total_sems = take(6)
+    shift_send, shift_recv, pair_sems, vec_send, vec_recv = take(5)
+
     me = lax.axis_index("expert")
     other = {"dp": 1 - lax.axis_index("dp")}
     section = lax.axis_index("section")
     after = {"section": lax.rem(section + 1, 4)}
     ahead = {"section": lax.rem(section + 3, 4)}
-    own = (w_gate, w_up, w_down)
-    fars = tuple(far.at[at] for at in range(3))
+    half = near.shape[1]
+    cuts = (slice(0, FIRST), slice(FIRST, half))
 
     barrier = pltpu.get_barrier_semaphore()
 
@@ -241,6 +221,12 @@
 
     for device in (other, after, ahead):
         pl.semaphore_signal(barrier, inc=1, device_id=device, device_id_type=MESH)
+
+    near_moves = [
+        pltpu.make_async_copy(own_hbm[at], near.at[at], near_sems.at[at]) for at in range(3)
+    ]
+    for move in near_moves:
+        move.start()
 
     def block(of):
         return pl.ds(pl.multiple_of(of * BLOCK, BLOCK), BLOCK)
@@ -263,8 +249,8 @@
         return pltpu.make_async_copy(sources.at[block(me)], targets.at[block(me)], sem)
 
     def issue(sources, targets, send, recv, sem):
+        each(sources, targets, send, recv, lambda copy: copy.start())
         own_block(sources, targets, sem).start()
-        each(sources, targets, send, recv, lambda copy: copy.start())
 
     def arrive(sources, targets, send, recv, sem):
         own_block(sources, targets, sem).wait()
@@ -280,21 +266,59 @@
             back_out.at[at], back_in.at[at], back_send.at[at], back_recv.at[at], local.at[3 + at],
         )
 
+    weight_moves = [
+        [
+            remote(
+                own_hbm[at].at[cut],
+                far.at[at, cut],
+                far_send.at[turn, at],
+                far_recv.at[turn, at],
+                other,
+            )
+            for at in range(3)
+        ]
+        for turn, cut in enumerate(cuts)
+    ]
+    grad_moves = [
+        [
+            remote(
+                far_grads.at[at, cut],
+                there_grads.at[at, cut],
+                grad_send.at[turn, at],
+                grad_recv.at[turn, at],
+                other,
+            )
+            for at in range(3)
+        ]
+        for turn, cut in enumerate(cuts)
+    ]
+    total_moves = [
+        [
+            pltpu.make_async_copy(
+                there_grads.at[at, cut], totals[at].at[cut], total_sems.at[turn, at]
+            )
+            for at in range(3)
+        ]
+        for turn, cut in enumerate(cuts)
+    ]
+    mine = Piece([near.at[at] for at in range(3)], kept_near)
+    first = Piece([far.at[at, cuts[0]] for at in range(3)], kept_first)
+    last = Piece([far.at[at, cuts[1]] for at in range(3)], kept_last)
+
     gain_row = gain[...].astype(F32)
-    place(places_bwd, routes_bwd[...])
+    place(places_bwd, routes_bwd)
     normed = norm_rows(saved_in[...], gain_row)[2]
     pack(places_bwd, normed, out_blocks.at[0])
 
     pl.semaphore_wait(barrier, EXPERTS + 2)
+    for move in weight_moves[0]:
+        move.start()
     issue(*outward(0))
-    weight_moves = [
-        remote(own[at], fars[at], far_send.at[at], far_recv.at[at], other) for at in range(3)
-    ]
-    for move in weight_moves:
+    for move in weight_moves[1]:
         move.start()
     pack(places_bwd, out_grad[...], out_blocks.at[1])
     issue(*outward(1))
-    place(places_fwd, routes_fwd[...])
+    place(places_fwd, routes_fwd)
     normed = norm_rows(fwd_in[...], gain_row)[2]
     pack(places_fwd, normed, out_blocks.at[2])
 
@@ -303,11 +327,25 @@
     def gates(of):
         logits = dot(of[...], router[...], 1, 1)
         return jax.nn.sigmoid(jnp.sum(jnp.where(lanes == me, logits, 0.0), axis=1, keepdims=True))
+
+    def send_grads(piece, turn):
+        cut = cuts[turn]
+        factors = ((piece.grad_gate, rows), (piece.grad_up, rows), (piece.hidden, scaled))
+        for at, (left, right) in enumerate(factors):
+            weight_grad(left, right, far_grads.at[at, cut], None)
+            grad_moves[turn][at].start()
 
     arrive(*outward(0))
     issue(*outward(2))
     unpack(in_blocks.at[0], rows)
     gate_bwd = gates(rows)
+    for move in near_moves:
+        move.wait()
+    pre_activate(rows, mine)
+    for move in weight_moves[0]:
+        move.wait()
+    pre_activate(rows, first)
+
     arrive(*outward(1))
     unpack(in_blocks.at[1], scaled)
 
@@ -315,62 +353,62 @@
     def _(cols):
         scaled[:, cols] = (gate_bwd * scaled[:, cols].astype(F32)).astype(BF16)
 
-    def half(weights, at, add):
-        return backward_half(
-            rows, scaled, weights, hidden.at[at], grad_gate.at[at], grad_up.at[at], grad_rows, add
-        )
-
-    share = half(own, 0, False)
-    for move in weight_moves:
+    share = backward_piece(scaled, first)
+    send_grads(first, 0)
+    share = share + backward_piece(scaled, mine)
+    row_grads(first, grad_rows, False)
+    row_grads(mine, grad_rows, True)
+    for move in weight_moves[1]:
         move.wait()
-    share = share + half(fars, 1, True)
-    grad_moves = [
-        remote(
-            far_grads.at[at], there_grads.at[at], grad_send.at[at], grad_recv.at[at], other
-        )
-        for at in range(3)
-    ]
-
-    factors = ((grad_gate, rows), (grad_up, rows), (hidden, scaled))
-    for at, (left, right) in enumerate(factors):
-        weight_grad(left.at[1], right, far_grads.at[at], None)
-        grad_moves[at].start()
+    pre_activate(rows, last)
+    share = share + backward_piece(scaled, last)
+    send_grads(last, 1)
+    row_grads(last, grad_rows, True)
 
     dlogit = (share * (1.0 - gate_bwd)).astype(BF16).astype(F32)
     row = lax.broadcasted_iota(jnp.int32, router.shape, 0)
-    mine = jnp.sum(jnp.where(row == me, router[...].astype(F32), 0.0), axis=0, keepdims=True)
+
+    @slabs()
+    def _(cols):
+        part = dlogit * jnp.sum(
+            jnp.where(row[:, 0:SLAB] == me, router[:, cols].astype(F32), 0.0),
+            axis=0,
+            keepdims=True,
+        )
+        grad_rows[:, cols] = grad_rows[:, cols] + part
+
+    repack(grad_rows, back_out.at[0])
+    issue(*homeward(0))
     for q in range(QUARTS):
         cols = slice(q * SLAB, (q + 1) * SLAB)
-        part = grad_rows[:, cols] + dlogit * mine[:, cols]
-        grad_rows[:, cols] = part
         rows_float = rows[:, cols].astype(F32)
         router_column = jnp.sum(rows_float * dlogit, axis=0, keepdims=True)
-        gain_part = jnp.sum(rows_float * part, axis=0, keepdims=True) / gain_row[:, cols]
+        gain_part = jnp.sum(rows_float * grad_rows[:, cols], axis=0, keepdims=True)
+        gain_part = gain_part / gain_row[:, cols]
         for at in range(4):
             vec[q * 4 + at : q * 4 + at + 1, :] = router_column[:, at * 128 : (at + 1) * 128]
             vec[16 + q * 4 + at : 17 + q * 4 + at, :] = gain_part[:, at * 128 : (at + 1) * 128]
-    repack(grad_rows, back_out.at[0])
-    issue(*homeward(0))
     pair = remote(vec, vec_other, pair_sems.at[0], pair_sems.at[1], other)
     pair.start()
 
     arrive(*outward(2))
     unpack(in_blocks.at[2], rows_fwd)
     gate_fwd = gates(rows_fwd)
-    for at, (gate, up, down) in enumerate((own, fars)):
-        pre_gate, pre_up = dot(rows_fwd[...], gate[...], 1, 1), dot(rows_fwd[...], up[...], 1, 1)
+    for at, weights in enumerate((near, far)):
+        pre_gate = dot(rows_fwd[...], weights[0], 1, 1)
+        pre_up = dot(rows_fwd[...], weights[1], 1, 1)
         fwd_hidden[...] = (pre_gate * jax.nn.sigmoid(pre_gate) * pre_up).astype(BF16)
 
         @slabs()
         def _(cols):
-            part = gate_fwd * dot(fwd_hidden[...], down[:, cols])
+            part = gate_fwd * dot(fwd_hidden[...], weights[2, :, cols])
             grad_rows[:, cols] = grad_rows[:, cols] + part if at else part
 
     repack(grad_rows, back_out.at[1])
     issue(*homeward(1))
 
     pair.wait()
-    vec_sum[...] = vec[...] + vec_other[...]
+    vec_sum[...] = (vec[...] + vec_other[...]).astype(BF16)
     vecs[me] = vec_sum[...]
 
     def share_vec(act):
@@ -388,6 +426,10 @@
 
     share_vec(lambda copy: copy.start())
 
+    near_factors = ((mine.grad_gate, rows), (mine.grad_up, rows), (mine.hidden, scaled))
+    for at, (left, right) in enumerate(near_factors):
+        weight_grad(left.at[:, cuts[1]], right, near_last.at[at], None)
+
     arrive(*homeward(0))
     dnormed = combine(places_bwd, back_in.at[0])
     x_bwd, inverse, _ = norm_rows(saved_in[...], gain_row)
@@ -398,6 +440,12 @@
     shift_bwd = remote(shift_out.at[0], sent_bwd, shift_send.at[0], shift_recv.at[0], ahead)
     shift_bwd.start()
 
+    for at, (left, right) in enumerate(near_factors):
+        there = there_grads.at[at, cuts[0]]
+        grad_moves[0][at].wait()
+        weight_grad(left.at[:, cuts[0]], right, there, there)
+        total_moves[0][at].start()
+
     arrive(*homeward(1))
     mixed = fwd_in[...].astype(F32) + combine(places_fwd, back_in.at[1])
     shift_out[1] = mixed.astype(BF16)
@@ -405,16 +453,19 @@
     shift_fwd.start()
 
     share_vec(lambda copy: copy.wait())
-    gain_total[...] = jnp.sum(vecs[:, 16:32, :], axis=0)
+    gain_total[...] = jnp.sum(vecs[:, 16:32, :].astype(F32), axis=0)
     for at in range(16):
-        router_total[:, at * 128 : (at + 1) * 128] = vecs[:, at, :]
-
-    totals = (total_gate, total_up, total_down)
-    for at, (left, right) in enumerate(factors):
-        grad_moves[at].wait()
-        weight_grad(left.at[0], right, totals[at], there_grads.at[at])
+        router_total[:, at * 128 : (at + 1) * 128] = vecs[:, at, :].astype(F32)
+    for at in range(3):
+        there = there_grads.at[at, cuts[1]]
+        grad_moves[1][at].wait()
+        there[...] = (near_last[at] + there[...].astype(F32)).astype(BF16)
+        total_moves[1][at].start()
     shift_bwd.wait()
     shift_fwd.wait()
+    for moves in total_moves:
+        for move in moves:
+            move.wait()
 
 
 def relay(*operands):
@@ -425,6 +476,7 @@
     pairs = EXPERTS * CAP
     vmem = pl.BlockSpec(memory_space=pltpu.VMEM)
     dma = pltpu.SemaphoreType.DMA
+    hbm = pl.BlockSpec(memory_space=pl.ANY)
     out_shape = [
         jax.ShapeDtypeStruct((tokens, width), BF16),
         jax.ShapeDtypeStruct((tokens, width), BF16),
@@ -434,6 +486,11 @@
         jax.ShapeDtypeStruct((EXPERTS, width), F32),
         jax.ShapeDtypeStruct((16, 128), F32),
     ]
+
+    def kept(units):
+        shape = (pairs, units)
+        return [pltpu.VMEM(shape, F32)] * 2 + [pltpu.VMEM(shape, BF16)] * 3
+
     scratch = [
         pltpu.VMEM((GROUPS, packed[0], QUARTS * tokens), BF16),
         pltpu.VMEM((GROUPS, packed[0], QUARTS * tokens), BF16),
@@ -443,9 +500,10 @@
         pltpu.VMEM((pairs, width), BF16),
         pltpu.VMEM((pairs, width), BF16),
         pltpu.VMEM((3, half, width), BF16),
-        pltpu.VMEM((2, pairs, half), BF16),
-        pltpu.VMEM((2, pairs, half), BF16),
-        pltpu.VMEM((2, pairs, half), BF16),
+        pltpu.VMEM((3, half, width), BF16),
+        *kept(half),
+        *kept(FIRST),
+        *kept(half - FIRST),
         pltpu.VMEM((pairs, half), BF16),
         pltpu.VMEM((pairs, width), F32),
         pltpu.VMEM((3, half, width), BF16),
@@ -453,19 +511,22 @@
         pltpu.VMEM((2,) + packed, BF16),
         pltpu.VMEM((2,) + packed, BF16),
         pltpu.VMEM((2, tokens, width), BF16),
+        pltpu.VMEM((3, half - FIRST, width), F32),
         pltpu.VMEM((32, 128), F32),
         pltpu.VMEM((32, 128), F32),
-        pltpu.VMEM((32, 128), F32),
-        pltpu.VMEM((EXPERTS, 32, 128), F32),
+        pltpu.VMEM((32, 128), BF16),
+        pltpu.VMEM((EXPERTS, 32, 128), BF16),
         dma((3, EXPERTS)),
         dma((3, EXPERTS)),
         dma((2, EXPERTS)),
         dma((2, EXPERTS)),
         dma((5,)),
         dma((3,)),
-        dma((3,)),
-        dma((3,)),
-        dma((3,)),
+        dma((2, 3)),
+        dma((2, 3)),
+        dma((2, 3)),
+        dma((2, 3)),
+        dma((2, 3)),
         dma((2,)),
         dma((2,)),
         dma((2,)),
@@ -475,8 +536,8 @@
     return pl.pallas_call(
         relay_kernel,
         out_shape=out_shape,
-        in_specs=[vmem] * len(operands),
-        out_specs=[vmem] * len(out_shape),
+        in_specs=[vmem] * 5 + [hbm] * 3 + [vmem] * 2,
+        out_specs=[hbm] * 5 + [vmem] * 2,
         scratch_shapes=scratch,
         compiler_params=pltpu.CompilerParams(
             collective_id=0, has_side_effects=True, vmem_limit_bytes=63 << 20
@@ -485,8 +546,41 @@
     )(*operands)
 
 
+def settle_kernel(*refs):
+    count = (len(refs) - 2) // 3
+    into, out_of = refs[-2], refs[-1]
+    loads = [
+        pltpu.make_async_copy(refs[at], refs[2 * count + at], into.at[at]) for at in range(count)
+    ]
+    stores = [
+        pltpu.make_async_copy(refs[2 * count + at], refs[count + at], out_of.at[at])
+        for at in range(count)
+    ]
+    for load in loads:
+        load.start()
+    for load, store in zip(loads, stores, strict=True):
+        load.wait()
+        store.start()
+    for store in stores:
+        store.wait()
+
+
+def settle(arrays):
+    hbm = pl.BlockSpec(memory_space=pl.ANY)
+    sems = pltpu.SemaphoreType.DMA((len(arrays),))
+    return pl.pallas_call(
+        settle_kernel,
+        out_shape=[jax.ShapeDtypeStruct(a.shape, a.dtype) for a in arrays],
+        in_specs=[hbm] * len(arrays),
+        out_specs=[hbm] * len(arrays),
+        scratch_shapes=[pltpu.VMEM(a.shape, a.dtype) for a in arrays] + [sems, sems],
+        compiler_params=pltpu.CompilerParams(vmem_limit_bytes=63 << 20),
+        name="settle",
+    )(*arrays)
+
+
 def shards(fwd_in, saved_in, out_grad, gain, router, w_gate, w_up, w_down, routes_fwd, routes_bwd):
-    sent_fwd, sent_bwd, total_gate, total_up, total_down, router_total, gain_total = relay(
+    results = relay(
         fwd_in[0],
         saved_in[0],
         out_grad[0],
@@ -495,9 +589,10 @@
         w_gate[0, 0].T,
         w_up[0, 0].T,
         w_down[0, 0],
-        routes_fwd[0],
-        routes_bwd[0],
+        routes_fwd[0].T,
+        routes_bwd[0].T,
     )
+    sent_fwd, sent_bwd, total_gate, total_up, total_down, router_total, gain_total = settle(results)
     return (
         sent_fwd[None],
         sent_bwd[None],

time: 246 us -> 229 us (0.931)
  local copies, waits for them, and re-layouts: 12.9 us -> 0 us
  Pallas kernels: 232 us -> 229 us
    unnamed x19 -> x0, local copies, waits for them, and re-layouts: 12.9 us -> none
    pallas_call x1 -> x2, Pallas kernels: 232 us -> 229 us  [the longest x1 224 us: relay(): pl.pallas_call(relay_kernel, out_shape=out_shape, in_specs=[vmem] * 5 + [...]
where the time goes in v2:
time: 229 us
  Pallas kernels  229 us (100%)
    pallas_call x1, Pallas kernels, relay(): pl.pallas_call(relay_kernel, out_shape=out_shape, in_specs=[vmem] * 5 + [...  224 us
    pallas_call x1, Pallas kernels, settle(): pl.pallas_call(settle_kernel, out_shape=[jax.ShapeDtypeStruct(a.shape, a....  4.9 us

profile of v2, /device:TPU:1, one launch (start us, length us, event | category | flops | bytes accessed | tf_op | source)
XLA Modules:
  0.0 229.3 jit_solution(6364494835471530838)
XLA Ops:
  0.6 223.6 %relay.1 = (bf16[128,2048]{1,0:T(8,128)(2,1)}, bf16[128,2048]{1,0:T(8,128)(2,1)}, bf16[352,2048]{1,0:T(8,128)(2,1)}, bf16[352,2048]{1,0:T(8,128)(2,1)}, bf16[352...) custom-call(bf16[128,2048]{1,0:T(8,128)(2,1)} %bitcast.35, bf16[128,2048]{1,0:T(8,128)(2,1)} %bitcast.36, ...), custom_call_target="tpu_custom_call" | custom-call | tf_op jit(solution)/shard_map/relay/pallas_call | solution.py:536
  224.3 4.9 %settle.1 = (bf16[128,2048]{1,0:T(8,128)(2,1)}, bf16[128,2048]{1,0:T(8,128)(2,1)}, bf16[352,2048]{1,0:T(8,128)(2,1)}, bf16[352,2048]{1,0:T(8,128)(2,1)}, bf16[35...) custom-call(bf16[128,2048]{1,0:T(8,128)(2,1)} %get-tuple-element.21.refs_0_, ...), custom_call_target="tpu_custom_call" | custom-call | tf_op jit(solution)/shard_map/settle/pallas_call | solution.py:571

commit v3 on v2

--- a/solution.py
+++ b/solution.py
@@ -163,15 +163,13 @@
         grad_rows[:, cols] = grad_rows[:, cols] + part if add else part
 
 
-def weight_grad(left, right, target, addend):
-    turned = left[...].T
+def weight_grad(left, right, left_there, right_there, target):
+    turned, turned_there = left[...].T, left_there[...].T
 
     @slabs()
     def _(cols):
-        part = dot(turned, right[:, cols])
-        if addend is not None:
-            part = part + addend[:, cols].astype(F32)
-        target[:, cols] = part.astype(target.dtype)
+        part = dot(turned, right[:, cols]) + dot(turned_there, right_there[:, cols])
+        target[:, cols] = part.astype(BF16)
 
 
 class Piece:
@@ -196,11 +194,12 @@
     router_total, gain_total = take(2)
     places_fwd, places_bwd, out_blocks, in_blocks, rows, scaled, rows_fwd, near, far = take(9)
     kept_near, kept_first, kept_last = take(5), take(5), take(5)
-    fwd_hidden, grad_rows, far_grads, there_grads, back_out, back_in, shift_out = take(7)
-    near_last = take(1)[0]
+    there_first, there_last = take(3), take(3)
+    there_rows, fwd_hidden, grad_rows, sums, back_out, back_in, shift_out = take(7)
     vec, vec_other, vec_sum, vecs = take(4)
     out_send, out_recv, back_send, back_recv, local = take(5)
     near_sems, far_send, far_recv, grad_send, grad_recv, total_sems = take(6)
+    row_send, row_recv = take(2)
     shift_send, shift_recv, pair_sems, vec_send, vec_recv = take(5)
 
     me = lax.axis_index("expert")
@@ -279,23 +278,23 @@
         ]
         for turn, cut in enumerate(cuts)
     ]
+    row_moves = [
+        remote(mine_rows, there_rows.at[at], row_send.at[at], row_recv.at[at], other)
+        for at, mine_rows in enumerate((rows, scaled))
+    ]
     grad_moves = [
         [
-            remote(
-                far_grads.at[at, cut],
-                there_grads.at[at, cut],
-                grad_send.at[turn, at],
-                grad_recv.at[turn, at],
-                other,
-            )
+            remote(kept[2 + at], there[at], grad_send.at[turn, at], grad_recv.at[turn, at], other)
             for at in range(3)
         ]
-        for turn, cut in enumerate(cuts)
+        for turn, (kept, there) in enumerate(
+            ((kept_first, there_first), (kept_last, there_last))
+        )
     ]
     total_moves = [
         [
             pltpu.make_async_copy(
-                there_grads.at[at, cut], totals[at].at[cut], total_sems.at[turn, at]
+                sums.at[at, cut], totals[(at + 2) % 3].at[cut], total_sems.at[turn, at]
             )
             for at in range(3)
         ]
@@ -328,16 +327,14 @@
         logits = dot(of[...], router[...], 1, 1)
         return jax.nn.sigmoid(jnp.sum(jnp.where(lanes == me, logits, 0.0), axis=1, keepdims=True))
 
-    def send_grads(piece, turn):
-        cut = cuts[turn]
-        factors = ((piece.grad_gate, rows), (piece.grad_up, rows), (piece.hidden, scaled))
-        for at, (left, right) in enumerate(factors):
-            weight_grad(left, right, far_grads.at[at, cut], None)
-            grad_moves[turn][at].start()
+    def send_grads(turn):
+        for move in grad_moves[turn]:
+            move.start()
 
     arrive(*outward(0))
     issue(*outward(2))
     unpack(in_blocks.at[0], rows)
+    row_moves[0].start()
     gate_bwd = gates(rows)
     for move in near_moves:
         move.wait()
@@ -353,8 +350,9 @@
     def _(cols):
         scaled[:, cols] = (gate_bwd * scaled[:, cols].astype(F32)).astype(BF16)
 
+    row_moves[1].start()
     share = backward_piece(scaled, first)
-    send_grads(first, 0)
+    send_grads(0)
     share = share + backward_piece(scaled, mine)
     row_grads(first, grad_rows, False)
     row_grads(mine, grad_rows, True)
@@ -362,7 +360,7 @@
         move.wait()
     pre_activate(rows, last)
     share = share + backward_piece(scaled, last)
-    send_grads(last, 1)
+    send_grads(1)
     row_grads(last, grad_rows, True)
 
     dlogit = (share * (1.0 - gate_bwd)).astype(BF16).astype(F32)
@@ -426,10 +424,6 @@
 
     share_vec(lambda copy: copy.start())
 
-    near_factors = ((mine.grad_gate, rows), (mine.grad_up, rows), (mine.hidden, scaled))
-    for at, (left, right) in enumerate(near_factors):
-        weight_grad(left.at[:, cuts[1]], right, near_last.at[at], None)
-
     arrive(*homeward(0))
     dnormed = combine(places_bwd, back_in.at[0])
     x_bwd, inverse, _ = norm_rows(saved_in[...], gain_row)
@@ -440,12 +434,26 @@
     shift_bwd = remote(shift_out.at[0], sent_bwd, shift_send.at[0], shift_recv.at[0], ahead)
     shift_bwd.start()
 
-    for at, (left, right) in enumerate(near_factors):
-        there = there_grads.at[at, cuts[0]]
-        grad_moves[0][at].wait()
-        weight_grad(left.at[:, cuts[0]], right, there, there)
-        total_moves[0][at].start()
-
+    rights = ((scaled, there_rows.at[1]), (rows, there_rows.at[0]), (rows, there_rows.at[0]))
+    lefts = (mine.hidden, mine.grad_gate, mine.grad_up)
+    for move in row_moves:
+        move.wait()
+
+    def finish(turn):
+        cut = cuts[turn]
+        there = (there_first, there_last)[turn]
+        for at in range(3):
+            grad_moves[turn][at].wait()
+            weight_grad(
+                lefts[at].at[:, cut],
+                rights[at][0],
+                there[at],
+                rights[at][1],
+                sums.at[at, cut],
+            )
+            total_moves[turn][at].start()
+
+    finish(0)
     arrive(*homeward(1))
     mixed = fwd_in[...].astype(F32) + combine(places_fwd, back_in.at[1])
     shift_out[1] = mixed.astype(BF16)
@@ -456,11 +464,7 @@
     gain_total[...] = jnp.sum(vecs[:, 16:32, :].astype(F32), axis=0)
     for at in range(16):
         router_total[:, at * 128 : (at + 1) * 128] = vecs[:, at, :].astype(F32)
-    for at in range(3):
-        there = there_grads.at[at, cuts[1]]
-        grad_moves[1][at].wait()
-        there[...] = (near_last[at] + there[...].astype(F32)).astype(BF16)
-        total_moves[1][at].start()
+    finish(1)
     shift_bwd.wait()
     shift_fwd.wait()
     for moves in total_moves:
@@ -504,14 +508,15 @@
         *kept(half),
         *kept(FIRST),
         *kept(half - FIRST),
+        *kept(FIRST)[2:],
+        *kept(half - FIRST)[2:],
+        pltpu.VMEM((2, pairs, width), BF16),
         pltpu.VMEM((pairs, half), BF16),
         pltpu.VMEM((pairs, width), F32),
-        pltpu.VMEM((3, half, width), BF16),
         pltpu.VMEM((3, half, width), BF16),
         pltpu.VMEM((2,) + packed, BF16),
         pltpu.VMEM((2,) + packed, BF16),
         pltpu.VMEM((2, tokens, width), BF16),
-        pltpu.VMEM((3, half - FIRST, width), F32),
         pltpu.VMEM((32, 128), F32),
         pltpu.VMEM((32, 128), F32),
         pltpu.VMEM((32, 128), BF16),
@@ -527,6 +532,8 @@
         dma((2, 3)),
         dma((2, 3)),
         dma((2, 3)),
+        dma((2,)),
+        dma((2,)),
         dma((2,)),
         dma((2,)),
         dma((2,)),

time: 229 us -> 220 us (0.961)
  Pallas kernels: 229 us -> 219 us
    pallas_call x1, Pallas kernels: 224 us -> 215 us  [relay(): pl.pallas_call(relay_kernel, out_shape=out_shape, in_specs=[vmem] * 5 + [...]
where the time goes in v3:
time: 220 us
  Pallas kernels  219 us (100%)
    pallas_call x1, Pallas kernels, relay(): pl.pallas_call(relay_kernel, out_shape=out_shape, in_specs=[vmem] * 5 + [...  215 us
    pallas_call x1, Pallas kernels, settle(): pl.pallas_call(settle_kernel, out_shape=[jax.ShapeDtypeStruct(a.shape, a....  4.9 us

profile of v3, /device:TPU:1, one launch (start us, length us, event | category | flops | bytes accessed | tf_op | source)
XLA Modules:
  0.0 220.3 jit_solution(5487464790304382905)
XLA Ops:
  0.6 214.6 %relay.1 = (bf16[128,2048]{1,0:T(8,128)(2,1)}, bf16[128,2048]{1,0:T(8,128)(2,1)}, bf16[352,2048]{1,0:T(8,128)(2,1)}, bf16[352,2048]{1,0:T(8,128)(2,1)}, bf16[352...) custom-call(bf16[128,2048]{1,0:T(8,128)(2,1)} %bitcast.35, bf16[128,2048]{1,0:T(8,128)(2,1)} %bitcast.36, ...), custom_call_target="tpu_custom_call" | custom-call | tf_op jit(solution)/shard_map/relay/pallas_call | solution.py:543
  215.2 4.9 %settle.1 = (bf16[128,2048]{1,0:T(8,128)(2,1)}, bf16[128,2048]{1,0:T(8,128)(2,1)}, bf16[352,2048]{1,0:T(8,128)(2,1)}, bf16[352,2048]{1,0:T(8,128)(2,1)}, bf16[35...) custom-call(bf16[128,2048]{1,0:T(8,128)(2,1)} %get-tuple-element.21.refs_0_, ...), custom_call_target="tpu_custom_call" | custom-call | tf_op jit(solution)/shard_map/settle/pallas_call | solution.py:578
